TPU v7x, 32 devices: a whole 2x2x4 slice. The times are simulated.
32 devices in a mesh: groups: 2 (over x), corpus: 16 (over z, y, core).
Axes of the slice: x: 2, y: 2, z: 4, core: 2. Of those that a mesh axis runs over, the one named last changes fastest.
Arguments:
- queries: float32 [1024, 8192], P(('groups', 'corpus')), parts along dimension 0, may hold values from -6 to 6
- hinv_slots: float32 [32, 4096, 512], P(('groups', 'corpus')), parts along dimension 0, may hold values from -0.09375 to 0.09375
- block_of: int32 [32], P('groups'), parts along dimension 0, may hold values from 0 to 15, each once
- corpus_enc: bfloat16 [16384, 8192], P(('groups', 'corpus')), parts along dimension 0, may hold values from -0.0625 to 0.0625
Outputs:
- scores: float32 [512, 16384], P(None, ('groups', 'corpus')), parts along dimension 1
There are 2 independent parts, one for each index of `groups`. A program takes and returns all parts, laid end to end along the dimension named above; each array names one. Nothing has to cross between parts.
Inputs may be any that keep to these rules, and one draw needn't show every extreme that they name: block_of names every column block exactly once.
All inputs are finite; a program needn't handle non-finite values.
Results may differ from a plain program's by a relative error of at most 0.003.
Values may be sent and summed in bfloat16 or wider, within the bound.
A program may use at most 128 MiB of HBM per device.

v0:
```python
import jax
import jax.numpy as jnp
from jax import lax
from jax.sharding import PartitionSpec as P


def on_device(queries, hinv_slots, block_of, corpus_enc):
    rows, width = queries.shape
    mod_width = hinv_slots.shape[1]
    block_width = hinv_slots.shape[2]
    per_module = mod_width // block_width
    modules = width // mod_width
    slots = block_of.shape[0]
    owners = block_of // per_module
    select = (owners[:, None] == jnp.arange(modules)[None, :]).astype(jnp.float32)
    outgoing = jnp.einsum(
        "km,rmi->kri",
        select,
        queries.reshape(rows, modules, mod_width),
        precision=lax.Precision.HIGHEST,
    )
    incoming = lax.all_to_all(outgoing, "corpus", split_axis=0, concat_axis=0, tiled=True)
    column_part = jnp.dot(
        incoming.reshape(-1, mod_width), hinv_slots[0], precision=lax.Precision.HIGHEST
    ).astype(jnp.bfloat16)
    returned = lax.all_to_all(column_part, "corpus", split_axis=0, concat_axis=1, tiled=True)
    placing = (block_of[:, None] == jnp.arange(slots)[None, :]).astype(jnp.float32)
    placed = jnp.einsum(
        "rsj,sb->rbj",
        returned.reshape(rows, slots, block_width).astype(jnp.float32),
        placing,
        precision=lax.Precision.HIGHEST,
    )
    precond = placed.reshape(rows, width).astype(jnp.bfloat16)
    return lax.dot_general(
        lax.all_gather(precond, "corpus", axis=0, tiled=True),
        corpus_enc,
        (((1,), (1,)), ((), ())),
        preferred_element_type=jnp.float32,
    )


def solution(mesh):
    return jax.shard_map(
        on_device,
        mesh=mesh,
        in_specs=(
            P(("groups", "corpus"), None),
            P(("groups", "corpus"), None, None),
            P("groups"),
            P(("groups", "corpus"), None),
        ),
        out_specs=P(None, ("groups", "corpus")),
        check_vma=False,
    )
```

profile of v0, /device:TPU:1, one launch (start us, length us, event | category | flops | bytes accessed | tf_op | source)
XLA Modules:
  0.0 336.8 jit_solution(783310543267607790)
XLA Ops:
  6.5 0.0 all-gather.2.cloned.1.call-start
  6.5 0.7 and_select_fusion
  7.2 2.1 reshape.15
  9.3 4.0 %fusion.10 = f32[16,32,4096]{2,0,1:T(8,128)S(1)} fusion(f32[32,2,4096]{2,1,0:T(2,128)S(1)} %reshape.15, s32[16]{0:T(128)S(1)} %and_select_fusion), kind=kOutput, calls=%fused_computation.9 | convolution fusion | flops 50331680 | bytes 9437248 | tf_op jit(solution)/shard_map/km,rmi->kri/dot_general | solution.py:16
  13.3 4.9 %copy.8 = f32[16,32,4096]{2,1,0:T(8,128)S(1)} copy(f32[16,32,4096]{2,0,1:T(8,128)S(1)} %fusion.10) | data formatting | bytes 16777216 | tf_op jit(solution)/shard_map/km,rmi->kri/dot_general | solution.py:16
  18.1 189.6 %all_to_all.21 = f32[16,32,4096]{2,1,0:T(8,128)S(1)} all-to-all(f32[16,32,4096]{2,1,0:T(8,128)S(1)} %copy.8), channel_id=1, replica_groups=mesh['groups'=2,'corpus'=16] {'corpus'}, dimensions={0} | all-to-all | bytes 16777216 | tf_op jit(solution)/shard_map/all_to_all | solution.py:22
  207.8 0.0 copy-start
  207.8 15.5 %fusion.2 = bf16[512,512]{1,0:T(8,128)(2,1)S(1)} fusion(f32[512,4096]{1,0:T(8,128)S(1)} %bitcast.23, f32[1,4096,512]{2,1,0:T(8,128)} %param.5), kind=kOutput, calls=%fused_computation.2 | convolution fusion | flops 12885164032 | bytes 17301504 | tf_op jit(solution)/shard_map/dot_general | solution.py:23
  223.3 19.2 %all_to_all.22 = bf16[16,32,512]{2,1,0:T(8,128)(2,1)S(1)} all-to-all(bf16[16,32,512]{2,1,0:T(8,128)(2,1)S(1)} %bitcast.24), channel_id=1, replica_groups=mesh['groups'=2,'corpus'=16] {'corpus'}, dimensions={0} | all-to-all | bytes 1048576 | tf_op jit(solution)/shard_map/all_to_all | solution.py:26
  242.5 0.0 copy-done
  242.5 0.4 convolution_convert_fusion
  242.9 1.1 copy.10
  244.0 0.0 all-gather.2.cloned.1.call-update
  244.0 74.7 %all-gather.2.cloned.1.call-done = bf16[512,8192]{1,0:T(8,128)(2,1)} async-done(((bf16[32,8192]{1,0:T(8,128)(2,1)}), bf16[512,8192]{1,0:T(8,128)(2,1)}) %all-gather.2.cloned.1.call-update) | async-done | bytes 8388624 | tf_op jit(solution)/shard_map/all_gather | solution.py:36
  318.7 11.3 %fusion.15 = f32[512,512]{1,0:T(8,128)} fusion(bf16[512,8192]{1,0:T(8,128)(2,1)} %all-gather.2.cloned.1.call-done, bf16[512,8192]{1,0:T(8,128)(2,1)} %param.7), kind=kOutput, calls=%fused_computation.18 | convolution fusion | flops 4294967296 | bytes 17825792 | tf_op jit(solution)/shard_map/dot_general | solution.py:35
Async XLA Ops:
  6.5 312.2 %all-gather.2.cloned.1.call-start = ((), (), s32[]{:S(2)}) async-start(), calls=%async_computation.2 | async-start | bytes 8912896 | tf_op jit(solution)/shard_map/all_gather | solution.py:36
  207.8 34.7 %copy-start = (s32[16]{0:T(128)S(1)}, s32[16]{0:T(128)}, u32[]{:S(2)}) copy-start(s32[16]{0:T(128)} %param.6) | copy-start | bytes 196
Sparse Core Ops, SparseCore 0:
  244.2 74.5 all-gather.1
where the time goes:
time: 337 us
  blocking collectives  209 us (62%)
  waiting for transfers between devices  74.7 us (22%)
  matrix products  31.1 us (9%)
  between operations  13.4 us (4%)
  local copies, waits for them, and re-layouts  8.06 us (2%)
    all_to_all x1, blocking collectives, on_device(): lax.all_to_all(outgoing, 'corpus', split_axis=0, concat_axis=0, tiled=True)  190 us
    all_gather x1, waiting for transfers between devices, on_device(): lax.all_gather(precond, 'corpus', axis=0, tiled=True)  74.7 us
    all_to_all x1, blocking collectives, on_device(): lax.all_to_all(column_part, 'corpus', split_axis=0, concat_axis=1, tiled=...  19.2 us
    dot_general x1, matrix products, on_device(): jnp.dot(incoming.reshape(-1, mod_width), hinv_slots[0], precision=lax.Pre...  15.5 us
    dot_general x1, matrix products, on_device(): lax.dot_general(lax.all_gather(precond, 'corpus', axis=0, tiled=True), co...  11.3 us
  transfers between devices with their start and end apart: 1, of which 1 were waited for; matrix products, arithmetic and copies ran while one was open for 0% of the time, Pallas kernels for 0%

commit v1 on v0

v1 whole, which is shorter than its diff:
```python
import jax
import jax.numpy as jnp
from jax import lax
from jax.experimental import pallas as pl
from jax.experimental.pallas import tpu as pltpu
from jax.sharding import PartitionSpec as P

RING = 8
PARTS = 4
MESH = pl.DeviceIdType.MESH


def by_collectives(queries, hinv_slots, block_of, corpus_enc):
    width = queries.shape[1]
    mod_width = hinv_slots.shape[1]
    block_width = hinv_slots.shape[2]
    per_module = mod_width // block_width
    slots = block_of.shape[0]
    me = lax.axis_index("corpus")
    gathered = lax.all_gather(queries.astype(jnp.bfloat16), "corpus", axis=0, tiled=True)
    order = jnp.arange(slots, dtype=block_of.dtype)
    my_block = jnp.sum(jnp.where(order == me, block_of, 0))
    mine = jnp.where(
        my_block // per_module == 0, gathered[:, :mod_width], gathered[:, mod_width:]
    )
    block = hinv_slots[0]
    high = block.astype(jnp.bfloat16)
    low = (block - high.astype(jnp.float32)).astype(jnp.bfloat16)
    part = jnp.dot(mine, high, preferred_element_type=jnp.float32)
    part += jnp.dot(mine, low, preferred_element_type=jnp.float32)
    parts = lax.all_gather(part.astype(jnp.bfloat16), "corpus", axis=0)
    placing = (block_of[:, None] == order[None, :]).astype(jnp.bfloat16)
    precond = jnp.einsum(
        "srj,sb->rbj", parts, placing, preferred_element_type=jnp.float32
    ).astype(jnp.bfloat16).reshape(-1, width)
    return lax.dot_general(
        precond, corpus_enc, (((1,), (1,)), ((), ())), preferred_element_type=jnp.float32
    )


def kernel(
    block_of, q_hbm, h_hbm, c_hbm, out,
    q_wide, h_wide, h_high, h_low, corpus, qbuf, pbuf, acc,
    load_sem, corpus_sem, q_ring_send, q_ring_recv, q_pair_send, q_pair_recv,
    p_ring_send, p_ring_recv, p_pair_send, p_pair_recv,
):
    rows = q_hbm.shape[0]
    mod_width, block_width = h_hbm.shape[1], h_hbm.shape[2]
    per_module = mod_width // block_width
    half = rows // 2
    depth = mod_width // PARTS
    part_rows = pbuf.shape[1] // PARTS

    me = lax.axis_index("corpus")
    core = me % 2
    across = (me // 2) % 2
    along = me // 4
    pos = along + across * (RING - 1 - 2 * along)

    def device(position, which):
        position = (position + 2 * RING) % RING
        y = position // (RING // 2)
        z = position + y * (RING - 1 - 2 * position)
        return z * 4 + y * 2 + which

    ahead = device(pos + 1 - 2 * core, core)
    behind = device(pos - 1 + 2 * core, core)
    pair = me + 1 - 2 * core

    load_q = pltpu.make_async_copy(q_hbm, q_wide, load_sem.at[0])
    load_q.start()
    load_h = [
        pltpu.make_async_copy(
            h_hbm.at[0, pl.ds(k * depth, depth)], h_wide.at[pl.ds(k * depth, depth)], load_sem.at[1 + k]
        )
        for k in range(PARTS)
    ]
    for copy in load_h:
        copy.start()
    slots = corpus.shape[0]
    load_c = [
        pltpu.make_async_copy(
            c_hbm.at[:, pl.ds(b * block_width, block_width)], corpus.at[b], corpus_sem.at[b]
        )
        for b in range(slots)
    ]
    for copy in load_c:
        copy.start()

    barrier = pltpu.get_barrier_semaphore()
    for other in (ahead, behind, pair):
        pl.semaphore_signal(barrier, inc=1, device_id={"corpus": other}, device_id_type=MESH)

    load_q.wait()
    for j in range(2):
        qbuf[j, core] = q_wide[:, j * mod_width:(j + 1) * mod_width].astype(jnp.bfloat16)
    out[...] = jnp.zeros_like(out)
    pl.semaphore_wait(barrier, 3)

    def q_piece(slot, k):
        return qbuf.at[k // 2, slot, pl.ds((k % 2) * half, half)]

    def q_ring(s, k):
        return pltpu.make_async_remote_copy(
            src_ref=q_piece(2 * s + core, k), dst_ref=q_piece(2 * s + 2 + core, k),
            send_sem=q_ring_send.at[s, k], recv_sem=q_ring_recv.at[s, k],
            device_id={"corpus": ahead}, device_id_type=MESH,
        )

    def q_pair(s, k, which):
        return pltpu.make_async_remote_copy(
            src_ref=q_piece(2 * s + which, k), dst_ref=q_piece(2 * s + which, k),
            send_sem=q_pair_send.at[s, k], recv_sem=q_pair_recv.at[s, k],
            device_id={"corpus": pair}, device_id_type=MESH,
        )

    def p_piece(slot, k):
        return pbuf.at[slot, pl.ds(k * part_rows, part_rows)]

    def p_ring(s, k):
        return pltpu.make_async_remote_copy(
            src_ref=p_piece(2 * s + core, k), dst_ref=p_piece(2 * s + 2 + core, k),
            send_sem=p_ring_send.at[s, k], recv_sem=p_ring_recv.at[s, k],
            device_id={"corpus": ahead}, device_id_type=MESH,
        )

    def p_pair(s, k, which):
        return pltpu.make_async_remote_copy(
            src_ref=p_piece(2 * s + which, k), dst_ref=p_piece(2 * s + which, k),
            send_sem=p_pair_send.at[s, k], recv_sem=p_pair_recv.at[s, k],
            device_id={"corpus": pair}, device_id_type=MESH,
        )

    for k in range(PARTS):
        q_ring(0, k).start()
    for k in range(PARTS):
        q_pair(0, k, core).start()

    for k in range(PARTS):
        load_h[k].wait()

        def split(i, carry, k=k):
            at = pl.ds(pl.multiple_of(k * depth + i * 128, 128), 128)
            wide = h_wide[at]
            high = wide.astype(jnp.bfloat16)
            h_high[at] = high
            h_low[at] = (wide - high.astype(jnp.float32)).astype(jnp.bfloat16)
            return carry

        lax.fori_loop(0, depth // 128, split, 0)

    second = (block_of[me] // per_module).astype(jnp.float32)
    weight = ((1.0 - second).astype(jnp.bfloat16), second.astype(jnp.bfloat16))

    def fold(s, k):
        pick = (
            qbuf[0, pl.ds(2 * s, 2), :, k * depth:(k + 1) * depth] * weight[0]
            + qbuf[1, pl.ds(2 * s, 2), :, k * depth:(k + 1) * depth] * weight[1]
        ).reshape(2 * rows, depth)
        at = slice(k * depth, (k + 1) * depth)
        total = jnp.dot(pick, h_high[at], preferred_element_type=jnp.float32)
        total += jnp.dot(pick, h_low[at], preferred_element_type=jnp.float32)
        if k == 0:
            acc[...] = total
        elif k < PARTS - 1:
            acc[...] += total
        else:
            at = pl.ds(pl.multiple_of(s * 2 * rows, 2 * rows), 2 * rows)
            pbuf[core, at] = (acc[...] + total).astype(jnp.bfloat16)

    def pair_arrived(s):
        for k in range(PARTS):
            q_pair(s, k, 1 - core).wait_recv()

    def q_step(s, carry):
        pair_arrived(s - 1)
        for k in range(PARTS):
            q_ring(s - 1, k).wait_recv()
            q_ring(s, k).start()
            q_pair(s, k, core).start()
            fold(s - 1, k)
        return carry

    lax.fori_loop(1, RING - 1, q_step, 0)

    for k in range(PARTS - 1):
        p_ring(0, k).start()
        p_pair(0, k, core).start()
    last = RING - 1
    pair_arrived(last - 1)
    for k in range(PARTS):
        q_ring(last - 1, k).wait_recv()
        q_pair(last, k, core).start()
        fold(last - 1, k)
    pair_arrived(last)
    for k in range(PARTS):
        fold(last, k)
    p_ring(0, PARTS - 1).start()
    p_pair(0, PARTS - 1, core).start()
    for copy in load_c:
        copy.wait()

    def score(s, which):
        origin = pos - s + 2 * s * which
        block = block_of[device(origin, which)]
        result = lax.dot_general(
            pbuf[2 * s + which], corpus[block], (((1,), (1,)), ((), ())),
            preferred_element_type=jnp.float32,
        )
        for t in range(RING):
            for w in range(2):
                row = device(origin - t + 2 * t * w, w) * rows
                cut = (2 * t + w) * rows
                out[pl.ds(pl.multiple_of(row, rows), rows)] += result[cut:cut + rows]

    def p_arrived(s):
        for k in range(PARTS):
            p_pair(s, k, 1 - core).wait_recv()

    def p_step(s, carry):
        for k in range(PARTS):
            p_ring(s - 1, k).wait_recv()
            p_ring(s, k).start()
            p_pair(s, k, core).start()
            if k == 1:
                score(s - 1, core)
        p_arrived(s - 1)
        score(s - 1, 1 - core)
        return carry

    lax.fori_loop(1, RING - 1, p_step, 0)
    for k in range(PARTS):
        p_ring(last - 1, k).wait_recv()
        p_pair(last, k, core).start()
        if k == 1:
            score(last - 1, core)
    p_arrived(last - 1)
    score(last - 1, 1 - core)
    score(last, core)
    p_arrived(last)
    score(last, 1 - core)

    def sent(s, carry):
        for k in range(PARTS):
            q_pair(s, k, core).wait_send()
            p_pair(s, k, core).wait_send()
        return carry

    def ring_sent(s, carry):
        for k in range(PARTS):
            q_ring(s, k).wait_send()
            p_ring(s, k).wait_send()
        return carry

    lax.fori_loop(0, RING, sent, 0)
    lax.fori_loop(0, RING - 1, ring_sent, 0)


def by_kernel(queries, hinv_slots, block_of, corpus_enc):
    rows, width = queries.shape
    _, mod_width, block_width = hinv_slots.shape
    held = corpus_enc.shape[0]
    slots = 2 * RING
    total = slots * rows
    sems = pltpu.SemaphoreType.DMA((RING, PARTS))
    anywhere = pl.BlockSpec(memory_space=pl.ANY)
    return pl.pallas_call(
        kernel,
        out_shape=jax.ShapeDtypeStruct((total, held), jnp.float32),
        in_specs=[pl.BlockSpec(memory_space=pltpu.SMEM), anywhere, anywhere, anywhere],
        out_specs=pl.BlockSpec(memory_space=pltpu.VMEM),
        scratch_shapes=[
            pltpu.VMEM((rows, width), jnp.float32),
            pltpu.VMEM((mod_width, block_width), jnp.float32),
            pltpu.VMEM((mod_width, block_width), jnp.bfloat16),
            pltpu.VMEM((mod_width, block_width), jnp.bfloat16),
            pltpu.VMEM((slots, held, block_width), jnp.bfloat16),
            pltpu.VMEM((2, slots, rows, mod_width), jnp.bfloat16),
            pltpu.VMEM((slots, total, block_width), jnp.bfloat16),
            pltpu.VMEM((2 * rows, block_width), jnp.float32),
            pltpu.SemaphoreType.DMA((1 + PARTS,)),
            pltpu.SemaphoreType.DMA((slots,)),
        ] + [sems] * 8,
        compiler_params=pltpu.CompilerParams(
            collective_id=0, has_side_effects=True, vmem_limit_bytes=58 * 2**20
        ),
        cost_estimate=pl.CostEstimate(
            flops=2 * total * block_width * mod_width * 2 + 2 * total * held * width,
            bytes_accessed=20 * 2**20, transcendentals=0,
        ),
    )(block_of, queries, hinv_slots, corpus_enc)


def solution(mesh):
    devices = mesh.shape["corpus"]

    def on_device(queries, hinv_slots, block_of, corpus_enc):
        fits = (
            devices == 2 * RING
            and queries.shape[0] % 32 == 0
            and queries.shape[1] == 2 * hinv_slots.shape[1]
            and hinv_slots.shape[2] % 128 == 0
        )
        body = by_kernel if fits else by_collectives
        return body(queries, hinv_slots, block_of, corpus_enc)

    return jax.shard_map(
        on_device,
        mesh=mesh,
        in_specs=(
            P(("groups", "corpus"), None),
            P(("groups", "corpus"), None, None),
            P("groups"),
            P(("groups", "corpus"), None),
        ),
        out_specs=P(None, ("groups", "corpus")),
        check_vma=False,
    )
```

time: 337 us -> 95.4 us (0.28)
  blocking collectives: 209 us -> 0 us
  Pallas kernels: 0 us -> 92.9 us
  waiting for transfers between devices: 74.7 us -> 0 us
  matrix products: 31.1 us -> 0 us
  between operations: 13.4 us -> 0.01 us
  local copies, waits for them, and re-layouts: 8.06 us -> 2.26 us
    all_to_all x2 -> x0, blocking collectives: 209 us -> none  [the longest x1 190 us: on_device(): lax.all_to_all(outgoing, 'corpus', split_axis=0, concat_axis=0, tiled=True)]
    pallas_call x0 -> x1, Pallas kernels: none -> 92.9 us  [by_kernel(): pl.pallas_call(kernel, out_shape=jax.ShapeDtypeStruct((total, held), jnp....]
    all_gather x1 -> x0, waiting for transfers between devices: 74.7 us -> none  [on_device(): lax.all_gather(precond, 'corpus', axis=0, tiled=True)]
    dot_general x4 -> x0, matrix products: 31.1 us -> none  [the longest x1 15.5 us: on_device(): jnp.dot(incoming.reshape(-1, mod_width), hinv_slots[0], precision=lax.Pre...]
    dot_general x1 -> x0, local copies, waits for them, and re-layouts: 4.86 us -> none  [on_device(): jnp.einsum('km,rmi->kri', select, queries.reshape(rows, modules, mod_widt...]
  transfers between devices with their start and end apart: 1 -> 0, of which waited for: 1 -> 0; matrix products, arithmetic and copies ran while one was open for 0% -> 0% of each run, Pallas kernels for 0% -> 0%
where the time goes in v1:
time: 95.4 us; the launch traced here: 95.2 us
  Pallas kernels  92.9 us (97%)
  local copies, waits for them, and re-layouts  2.26 us (2%)
    pallas_call x1, Pallas kernels, by_kernel(): pl.pallas_call(kernel, out_shape=jax.ShapeDtypeStruct((total, held), jnp....  92.9 us
    unnamed x1, local copies, waits for them, and re-layouts  2.26 us

profile of v1, /device:TPU:1, one launch (start us, length us, event | category | flops | bytes accessed | tf_op | source)
XLA Modules:
  0.0 95.2 jit_solution(56753142457958957)
XLA Ops:
  0.0 92.9 %shard_map.46 = f32[512,512]{1,0:T(8,128)} custom-call(s32[16]{0:T(128)} %block_of.1, f32[32,8192]{1,0:T(8,128)} %q_hbm.1, f32[1,4096,512]{2,1,0:T(8,128)} %h_hbm.1, bf16[512,8192]{1,0:T(8,128)(2,1)} %c_hbm.1), custom_call_target="tpu_custom_call" | custom-call | flops 8589934592 | bytes 20971520 | tf_op jit(solution)/shard_map/pallas_call | solution.py:267
  92.9 2.3 %copy.6 = f32[512,512]{1,0:T(8,128)} copy(f32[512,512]{1,0:T(8,128)} %shard_map.46) | data formatting | bytes 2097152

commit v2 on v1

--- a/solution.py
+++ b/solution.py
@@ -67,16 +67,25 @@
     behind = device(pos - 1 + 2 * core, core)
     pair = me + 1 - 2 * core
 
-    load_q = pltpu.make_async_copy(q_hbm, q_wide, load_sem.at[0])
-    load_q.start()
+    load_q = [
+        pltpu.make_async_copy(
+            q_hbm.at[pl.ds((k % 2) * half, half), pl.ds((k // 2) * mod_width, mod_width)],
+            q_wide.at[pl.ds((k % 2) * half, half), pl.ds((k // 2) * mod_width, mod_width)],
+            load_sem.at[k],
+        )
+        for k in range(PARTS)
+    ]
+    for copy in load_q:
+        copy.start()
+    barrier = pltpu.get_barrier_semaphore()
+    for other in (ahead, behind, pair):
+        pl.semaphore_signal(barrier, inc=1, device_id={"corpus": other}, device_id_type=MESH)
     load_h = [
         pltpu.make_async_copy(
-            h_hbm.at[0, pl.ds(k * depth, depth)], h_wide.at[pl.ds(k * depth, depth)], load_sem.at[1 + k]
+            h_hbm.at[0, pl.ds(k * depth, depth)], h_wide.at[pl.ds(k * depth, depth)], load_sem.at[PARTS + k]
         )
         for k in range(PARTS)
     ]
-    for copy in load_h:
-        copy.start()
     slots = corpus.shape[0]
     load_c = [
         pltpu.make_async_copy(
@@ -84,18 +93,6 @@
         )
         for b in range(slots)
     ]
-    for copy in load_c:
-        copy.start()
-
-    barrier = pltpu.get_barrier_semaphore()
-    for other in (ahead, behind, pair):
-        pl.semaphore_signal(barrier, inc=1, device_id={"corpus": other}, device_id_type=MESH)
-
-    load_q.wait()
-    for j in range(2):
-        qbuf[j, core] = q_wide[:, j * mod_width:(j + 1) * mod_width].astype(jnp.bfloat16)
-    out[...] = jnp.zeros_like(out)
-    pl.semaphore_wait(barrier, 3)
 
     def q_piece(slot, k):
         return qbuf.at[k // 2, slot, pl.ds((k % 2) * half, half)]
@@ -132,14 +129,20 @@
         )
 
     for k in range(PARTS):
+        load_q[k].wait()
+        held_rows = slice((k % 2) * half, (k % 2 + 1) * half)
+        held_columns = slice((k // 2) * mod_width, (k // 2 + 1) * mod_width)
+        qbuf[k // 2, core, held_rows] = q_wide[held_rows, held_columns].astype(jnp.bfloat16)
+        if k == 0:
+            pl.semaphore_wait(barrier, 3)
         q_ring(0, k).start()
-    for k in range(PARTS):
         q_pair(0, k, core).start()
-
-    for k in range(PARTS):
-        load_h[k].wait()
-
-        def split(i, carry, k=k):
+    for copy in load_h + load_c:
+        copy.start()
+    out[...] = jnp.zeros_like(out)
+
+    def split_part(k):
+        def split(i, carry):
             at = pl.ds(pl.multiple_of(k * depth + i * 128, 128), 128)
             wide = h_wide[at]
             high = wide.astype(jnp.bfloat16)
@@ -181,7 +184,16 @@
             fold(s - 1, k)
         return carry
 
-    lax.fori_loop(1, RING - 1, q_step, 0)
+    for k in range(PARTS):
+        q_ring(0, k).wait_recv()
+        q_ring(1, k).start()
+        q_pair(1, k, core).start()
+        load_h[k].wait()
+        split_part(k)
+        if k == 0:
+            pair_arrived(0)
+        fold(0, k)
+    lax.fori_loop(2, RING - 1, q_step, 0)
 
     for k in range(PARTS - 1):
         p_ring(0, k).start()
@@ -200,21 +212,21 @@
     for copy in load_c:
         copy.wait()
 
-    def score(s, which):
+    def score(s, which, low=0, high=PARTS):
         origin = pos - s + 2 * s * which
         block = block_of[device(origin, which)]
+        start = low * part_rows
         result = lax.dot_general(
-            pbuf[2 * s + which], corpus[block], (((1,), (1,)), ((), ())),
+            pbuf[2 * s + which, start:high * part_rows], corpus[block], (((1,), (1,)), ((), ())),
             preferred_element_type=jnp.float32,
         )
-        for t in range(RING):
-            for w in range(2):
-                row = device(origin - t + 2 * t * w, w) * rows
-                cut = (2 * t + w) * rows
-                out[pl.ds(pl.multiple_of(row, rows), rows)] += result[cut:cut + rows]
-
-    def p_arrived(s):
-        for k in range(PARTS):
+        for i in range((high - low) * part_rows // rows):
+            t, w = (start // rows + i) // 2, i % 2
+            row = device(origin - t + 2 * t * w, w) * rows
+            out[pl.ds(pl.multiple_of(row, rows), rows)] += result[i * rows:(i + 1) * rows]
+
+    def p_arrived(s, low=0, high=PARTS):
+        for k in range(low, high):
             p_pair(s, k, 1 - core).wait_recv()
 
     def p_step(s, carry):
@@ -222,38 +234,46 @@
             p_ring(s - 1, k).wait_recv()
             p_ring(s, k).start()
             p_pair(s, k, core).start()
+            q_ring(s - 1, k).wait_send()
+            q_pair(s - 1, k, core).wait_send()
             if k == 1:
                 score(s - 1, core)
         p_arrived(s - 1)
         score(s - 1, 1 - core)
         return carry
 
-    lax.fori_loop(1, RING - 1, p_step, 0)
+    lax.fori_loop(1, last, p_step, 0)
+
+    def p_sent(s, carry):
+        for k in range(PARTS):
+            p_ring(s, k).wait_send()
+            p_pair(s, k, core).wait_send()
+        return carry
+
+    middle = PARTS // 2
     for k in range(PARTS):
         p_ring(last - 1, k).wait_recv()
         p_pair(last, k, core).start()
-        if k == 1:
+        if k == 0:
             score(last - 1, core)
-    p_arrived(last - 1)
-    score(last - 1, 1 - core)
-    score(last, core)
-    p_arrived(last)
-    score(last, 1 - core)
-
-    def sent(s, carry):
-        for k in range(PARTS):
-            q_pair(s, k, core).wait_send()
-            p_pair(s, k, core).wait_send()
-        return carry
-
-    def ring_sent(s, carry):
-        for k in range(PARTS):
-            q_ring(s, k).wait_send()
-            p_ring(s, k).wait_send()
-        return carry
-
-    lax.fori_loop(0, RING, sent, 0)
-    lax.fori_loop(0, RING - 1, ring_sent, 0)
+            for i in range(PARTS):
+                q_ring(last - 1, i).wait_send()
+                q_pair(last - 1, i, core).wait_send()
+                q_pair(last, i, core).wait_send()
+        elif k == 1:
+            p_arrived(last - 1)
+            score(last - 1, 1 - core)
+            lax.fori_loop(0, last - 2, p_sent, 0)
+        elif k == 2:
+            score(last, core, 0, middle)
+            p_arrived(last, 0, middle)
+            score(last, 1 - core, 0, middle)
+    score(last, core, middle, PARTS)
+    p_arrived(last, middle, PARTS)
+    score(last, 1 - core, middle, PARTS)
+    lax.fori_loop(last - 2, last, p_sent, 0)
+    for k in range(PARTS):
+        p_pair(last, k, core).wait_send()
 
 
 def by_kernel(queries, hinv_slots, block_of, corpus_enc):
@@ -266,7 +286,7 @@
     anywhere = pl.BlockSpec(memory_space=pl.ANY)
     return pl.pallas_call(
         kernel,
-        out_shape=jax.ShapeDtypeStruct((total, held), jnp.float32),
+        out_shape=pltpu.VMEM((total, held), jnp.float32),
         in_specs=[pl.BlockSpec(memory_space=pltpu.SMEM), anywhere, anywhere, anywhere],
         out_specs=pl.BlockSpec(memory_space=pltpu.VMEM),
         scratch_shapes=[
@@ -278,11 +298,11 @@
             pltpu.VMEM((2, slots, rows, mod_width), jnp.bfloat16),
             pltpu.VMEM((slots, total, block_width), jnp.bfloat16),
             pltpu.VMEM((2 * rows, block_width), jnp.float32),
-            pltpu.SemaphoreType.DMA((1 + PARTS,)),
+            pltpu.SemaphoreType.DMA((2 * PARTS,)),
             pltpu.SemaphoreType.DMA((slots,)),
         ] + [sems] * 8,
         compiler_params=pltpu.CompilerParams(
-            collective_id=0, has_side_effects=True, vmem_limit_bytes=58 * 2**20
+            collective_id=0, has_side_effects=True, vmem_limit_bytes=61 * 2**20
         ),
         cost_estimate=pl.CostEstimate(
             flops=2 * total * block_width * mod_width * 2 + 2 * total * held * width,

time: 95.4 us -> 91.3 us (0.957)
  Pallas kernels: 92.9 us -> 90.1 us
  local copies, waits for them, and re-layouts: 2.26 us -> 0.97 us
    pallas_call x1, Pallas kernels: 92.9 us -> 90.1 us  [by_kernel(): pl.pallas_call(kernel, out_shape=pltpu.VMEM((total, held), jnp.float32),...]
    unnamed x1, local copies, waits for them, and re-layouts: 2.26 us -> 0.97 us
where the time goes in v2:
time: 91.3 us; the launch traced here: 91.1 us
  Pallas kernels  90.1 us (99%)
  local copies, waits for them, and re-layouts  0.97 us (1%)
    pallas_call x1, Pallas kernels, by_kernel(): pl.pallas_call(kernel, out_shape=pltpu.VMEM((total, held), jnp.float32),...  90.1 us

profile of v2, /device:TPU:1, one launch (start us, length us, event | category | flops | bytes accessed | tf_op | source)
XLA Modules:
  0.0 91.1 jit_solution(10536457349252710409)
XLA Ops:
  0.0 90.1 %shard_map.46 = f32[512,512]{1,0:T(8,128)S(1)} custom-call(s32[16]{0:T(128)} %block_of.1, f32[32,8192]{1,0:T(8,128)} %q_hbm.1, f32[1,4096,512]{2,1,0:T(8,128)} %h_hbm.1, bf16[512,8192]{1,0:T(8,128)(2,1)} %c_hbm.1), custom_call_target="tpu_custom_call" | custom-call | flops 8589934592 | bytes 20971520 | tf_op jit(solution)/shard_map/pallas_call | solution.py:287
  90.2 1.0 %copy.6 = f32[512,512]{1,0:T(8,128)} copy(f32[512,512]{1,0:T(8,128)S(1)} %shard_map.46) | data formatting | bytes 2097152

commit v3 on v2

--- a/solution.py
+++ b/solution.py
@@ -67,6 +67,9 @@
     behind = device(pos - 1 + 2 * core, core)
     pair = me + 1 - 2 * core
 
+    barrier = pltpu.get_barrier_semaphore()
+    for other in (ahead, behind, pair):
+        pl.semaphore_signal(barrier, inc=1, device_id={"corpus": other}, device_id_type=MESH)
     load_q = [
         pltpu.make_async_copy(
             q_hbm.at[pl.ds((k % 2) * half, half), pl.ds((k // 2) * mod_width, mod_width)],
@@ -77,9 +80,6 @@
     ]
     for copy in load_q:
         copy.start()
-    barrier = pltpu.get_barrier_semaphore()
-    for other in (ahead, behind, pair):
-        pl.semaphore_signal(barrier, inc=1, device_id={"corpus": other}, device_id_type=MESH)
     load_h = [
         pltpu.make_async_copy(
             h_hbm.at[0, pl.ds(k * depth, depth)], h_wide.at[pl.ds(k * depth, depth)], load_sem.at[PARTS + k]
@@ -195,14 +195,15 @@
         fold(0, k)
     lax.fori_loop(2, RING - 1, q_step, 0)
 
+    last = RING - 1
     for k in range(PARTS - 1):
         p_ring(0, k).start()
-        p_pair(0, k, core).start()
-    last = RING - 1
     pair_arrived(last - 1)
     for k in range(PARTS):
         q_ring(last - 1, k).wait_recv()
         q_pair(last, k, core).start()
+        if k < PARTS - 1:
+            p_pair(0, k, core).start()
         fold(last - 1, k)
     pair_arrived(last)
     for k in range(PARTS):
@@ -264,14 +265,15 @@
             p_arrived(last - 1)
             score(last - 1, 1 - core)
             lax.fori_loop(0, last - 2, p_sent, 0)
+            score(last, core, 0, middle)
         elif k == 2:
-            score(last, core, 0, middle)
-            p_arrived(last, 0, middle)
-            score(last, 1 - core, 0, middle)
-    score(last, core, middle, PARTS)
+            p_arrived(last, 0, k)
+            score(last, 1 - core, 0, k)
+            lax.fori_loop(last - 2, last, p_sent, 0)
+            score(last, core, k, k + 1)
+    score(last, core, PARTS - 1, PARTS)
     p_arrived(last, middle, PARTS)
     score(last, 1 - core, middle, PARTS)
-    lax.fori_loop(last - 2, last, p_sent, 0)
     for k in range(PARTS):
         p_pair(last, k, core).wait_send()
 

time: 91.3 us -> 91.2 us (level)
  no operation moved by 1% of the time
where the time goes in v3:
time: 91.2 us; the launch traced here: 91.1 us
  Pallas kernels  90.1 us (99%)
  local copies, waits for them, and re-layouts  0.97 us (1%)
    pallas_call x1, Pallas kernels, by_kernel(): pl.pallas_call(kernel, out_shape=pltpu.VMEM((total, held), jnp.float32),...  90.1 us

profile of v3, /device:TPU:1, one launch (start us, length us, event | category | flops | bytes accessed | tf_op | source)
XLA Modules:
  0.0 91.1 jit_solution(6305810854715791637)
XLA Ops:
  0.0 90.1 %shard_map.46 = f32[512,512]{1,0:T(8,128)S(1)} custom-call(s32[16]{0:T(128)} %block_of.1, f32[32,8192]{1,0:T(8,128)} %q_hbm.1, f32[1,4096,512]{2,1,0:T(8,128)} %h_hbm.1, bf16[512,8192]{1,0:T(8,128)(2,1)} %c_hbm.1), custom_call_target="tpu_custom_call" | custom-call | flops 8589934592 | bytes 20971520 | tf_op jit(solution)/shard_map/pallas_call | solution.py:289
  90.1 1.0 %copy.6 = f32[512,512]{1,0:T(8,128)} copy(f32[512,512]{1,0:T(8,128)S(1)} %shard_map.46) | data formatting | bytes 2097152
